TPU v7x, 512 devices: a whole 4x8x8 slice. The times are simulated.
512 devices in a mesh: ha: 16 (over y, core), wa: 32 (over z, x).
Axes of the slice: x: 4, y: 8, z: 8, core: 2. Of those that a mesh axis runs over, the one named last changes fastest.
Arguments:
- volume: bfloat16 [4, 64, 256, 32], P(None, 'ha', 'wa'), may hold values from -6 to 6
- hidden_pre: bfloat16 [128, 64, 256, 32], P(None, 'ha', 'wa'), may hold values from -6 to 6
- grad_out: bfloat16 [128, 64, 256, 32], P(None, 'ha', 'wa'), may hold values from -0.008239746 to 0.008239746
- weight_two: bfloat16 [3, 3, 3, 128, 128], replicated, may hold values from -0.109375 to 0.109375
Outputs:
- grad_one: float32 [3, 3, 3, 4, 128], replicated
- grad_two: float32 [3, 3, 3, 128, 128], replicated
All inputs are finite; a program needn't handle non-finite values.
Results may differ from a plain program's by a relative error of at most 0.0034.
Values may be sent and summed in bfloat16 or wider, within the bound.
A program may use at most 64 MiB of HBM per device.

v0:
```python
import jax
import jax.numpy as jnp
from jax import lax
from jax.sharding import PartitionSpec as P


def padded_2(block, sides, width):
    for axis, dim in sides:
        count = lax.axis_size(axis)
        forward = [(i, i + 1) for i in range(count - 1)]
        backward = [(target, source) for source, target in forward]
        low = lax.ppermute(
            lax.slice_in_dim(block, block.shape[dim] - width, None, axis=dim), axis, forward
        )
        high = lax.ppermute(lax.slice_in_dim(block, 0, width, axis=dim), axis, backward)
        block = jnp.concatenate([low, block, high], axis=dim)
    return block


def kernel_terms(padded_in, local_out):
    in_chans = padded_in.shape[0]
    out_chans = local_out.shape[0]
    tall = local_out.shape[1]
    across = local_out.shape[2]
    depth = local_out.shape[3]
    flat_out = local_out.reshape(out_chans, tall * across * depth)
    pieces = []
    for shift_h in range(3):
        for shift_w in range(3):
            for shift_d in range(3):
                window = padded_in[
                    :,
                    shift_h : shift_h + tall,
                    shift_w : shift_w + across,
                    shift_d : shift_d + depth,
                ]
                window = window.reshape(in_chans, tall * across * depth)
                pieces.append(
                    jnp.einsum("cp,op->co", window, flat_out, preferred_element_type=jnp.float32)
                )
    return jnp.stack(pieces).reshape(3, 3, 3, in_chans, out_chans)


def body(volume, hidden_pre, grad_out, weight_two):
    in_count = volume.shape[0]
    chan_count = grad_out.shape[0]
    active = jnp.maximum(hidden_pre, jnp.zeros((), jnp.bfloat16))
    stacked = jnp.concatenate([volume, grad_out, active], axis=0)
    padded = padded_2(stacked, (("ha", 1), ("wa", 2)), 1)
    padded = jnp.pad(padded, ((0, 0), (0, 0), (0, 0), (1, 1)))
    volume_pad = padded[:in_count]
    grad_pad = padded[in_count : in_count + chan_count]
    active_pad = padded[in_count + chan_count :]
    grad_two = kernel_terms(active_pad, grad_out)
    grad_act = lax.conv_general_dilated(
        grad_pad[None],
        weight_two[::-1, ::-1, ::-1],
        (1, 1, 1),
        "VALID",
        dimension_numbers=("NCHWD", "HWDOI", "NCHWD"),
        preferred_element_type=jnp.float32,
    )[0]
    grad_hidden = (grad_act * (hidden_pre > 0).astype(jnp.float32)).astype(jnp.bfloat16)
    grad_one = kernel_terms(volume_pad, grad_hidden)
    grad_one, grad_two = lax.psum((grad_one, grad_two), ("ha", "wa"))
    return (grad_one, grad_two)


def solution(mesh):
    in_specs = (
        P(None, "ha", "wa", None),
        P(None, "ha", "wa", None),
        P(None, "ha", "wa", None),
        P(),
    )
    out_specs = (P(), P())
    return jax.shard_map(body, mesh=mesh, in_specs=in_specs, out_specs=out_specs, check_vma=False)
```

profile of v0, /device:TPU:1, one launch (start us, length us, event | category | flops | bytes accessed | tf_op | source)
XLA Modules:
  0.0 373.7 jit_solution(17802894344891257581)
XLA Ops:
  7.2 1.1 copy_maximum_fusion
  8.4 1.1 copy.130
  9.5 1.1 pad_maximum_fusion.16
  10.6 8.8 %collective-permute-start.1 = (bf16[260,1,8,32]{0,3,2,1:T(8,128)(2,1)S(1)}, bf16[260,1,8,32]{0,3,2,1:T(8,128)(2,1)S(1)}, u32[]{:S(2)}, u32[]{:S(2)}) collective-permute-start(bf16[260,1,8,32]{0,3,2,1:T(8,128)(2,1)S(1)} %get-tuple-element.7), channel_id=1, source_target_pairs={{32,0},{64,32},{96,64},{128,96},{160,128},{192,160},{224,192},{256... | collective-permute-start | bytes 399368 | tf_op jit(solution)/shard_map/ppermute | solution.py:15
  19.4 1.9 collective-permute-start
  21.4 2.6 collective-permute-done
  24.1 1.3 collective-permute-start.3
  25.4 4.6 %collective-permute-start.2 = (bf16[260,6,1,32]{0,3,2,1:T(8,128)(2,1)S(1)}, bf16[260,6,1,32]{0,3,2,1:T(8,128)(2,1)}, u32[]{:S(2)}, u32[]{:S(2)}) collective-permute-start(bf16[260,6,1,32]{0,3,2,1:T(8,128)(2,1)S(1)} %get-tuple-element.4), channel_id=1, source_target_pairs={{0,1},{1,2},{2,3},{3,4},{4,5},{5,6},{6,7},{7,8},{8,9},{9,10},{10,1... | collective-permute-start | bytes 299528 | tf_op jit(solution)/shard_map/ppermute | solution.py:12
  30.0 0.8 copy.207
  31.0 0.7 copy-done.7
  31.6 1.1 collective-permute-done.2
  32.7 1.4 pad_maximum_fusion
  34.1 3.2 copy.132
  37.3 4.1 %slice_bitcast_fusion = bf16[128,6,10,1,34]{4,0,2,1,3:T(8,128)(2,1)} fusion(bf16[260,6,10,32]{3,0,2,1:T(8,128)(2,1)} %copy.132), kind=kLoop, calls=%fused_computation | loop fusion | bytes 1520640 | tf_op jit(solution)/shard_map/broadcast_in_dim | solution.py:56
  41.4 3.3 pad.4
  44.7 2.2 copy.278
  47.6 2.5 convolution_select_fusion
  50.3 0.7 fusion.18
  51.3 2.4 pad_maximum_fusion.1
  56.1 0.5 fusion.49
  57.2 0.5 fusion.47
  59.4 0.5 fusion.43
  60.4 0.5 fusion.41
  61.7 0.9 fusion.17
  62.6 0.6 fusion.16
  63.6 0.9 fusion.15
  64.5 0.6 fusion.14
  65.5 0.9 fusion.13
  66.5 0.6 fusion.12
  67.5 0.9 fusion.11
  68.4 0.6 fusion.10
  69.4 0.9 fusion.9
  70.4 0.6 fusion.8
  71.4 0.9 fusion.7
  72.3 0.6 fusion.6
  73.3 1.1 fusion.5
  74.5 0.6 fusion.4
  75.4 0.9 fusion.3
  76.4 0.6 fusion.2
  77.4 0.9 fusion.1
  78.3 1.2 copy-done.4
  79.8 1.3 fusion.39
  81.1 1.2 fusion.38
  82.3 1.2 fusion.28
  83.5 1.3 fusion.37
  84.8 106.6 %psum.14 = f32[3,3,3,4,128]{4,3,2,1,0:T(4,128)} all-reduce(f32[3,3,3,4,128]{4,3,2,1,0:T(4,128)S(1)} %bitcast.483), channel_id=1, replica_groups=mesh['ha'=16,'wa'=32] {'ha','wa'}, use_global_device_ids=true, to_apply=%region_0.1 | all-reduce | flops 13824 | bytes 110592 | tf_op jit(solution)/shard_map/psum | solution.py:65
  191.4 172.5 %all-reduce.3.cloned.1.call-done = f32[3,3,3,128,128]{4,3,2,1,0:T(8,128)} async-done(((f32[3,3,3,128,128]{4,3,2,1,0:T(8,128)}), f32[3,3,3,128,128]{4,3,2,1,0:T(8,128)}) %all-reduce.3.cloned.1.call-update) | async-done | bytes 1769488 | tf_op jit(solution)/shard_map/psum | solution.py:65
  363.9 2.9 copy.389
  (61 shorter events, 10.6 us)
Async XLA Ops:
  7.2 40.1 %copy-start = (bf16[3,3,3,128,128]{4,3,2,1,0:T(8,128)(2,1)S(1)}, bf16[3,3,3,128,128]{4,3,2,1,0:T(8,128)(2,1)}, u32[]{:S(2)}) copy-start(bf16[3,3,3,128,128]{4,3,2,1,0:T(8,128)(2,1)} %param.7) | copy-start | bytes 2654212
  7.2 16.8 %copy-start.2 = (bf16[128,4,8,32]{0,3,2,1:T(8,128)(2,1)S(1)}, bf16[128,4,8,32]{0,3,2,1:T(8,128)(2,1)}, u32[]{:S(2)}) copy-start(bf16[128,4,8,32]{0,3,2,1:T(8,128)(2,1)} %param.6) | copy-start | bytes 786436
  7.2 356.7 %all-reduce.3.cloned.1.call-start = ((), (), s32[]{:S(2)}) async-start(), calls=%async_computation | async-start | bytes 3538944 | tf_op jit(solution)/shard_map/psum | solution.py:65
  8.4 21.7 %copy-start.9 = (bf16[4,4,8,32]{3,2,1,0:T(8,128)(2,1)S(1)}, bf16[4,4,8,32]{3,2,1,0:T(8,128)(2,1)}, u32[]{:S(2)}) copy-start(bf16[4,4,8,32]{3,2,1,0:T(8,128)(2,1)} %param.4) | copy-start | bytes 24580
  10.6 10.7 %collective-permute-start.1 = (bf16[260,1,8,32]{0,3,2,1:T(8,128)(2,1)S(1)}, bf16[260,1,8,32]{0,3,2,1:T(8,128)(2,1)S(1)}, u32[]{:S(2)}, u32[]{:S(2)}) collective-permute-start(bf16[260,1,8,32]{0,3,2,1:T(8,128)(2,1)S(1)} %get-tuple-element.7), channel_id=1, source_target_pairs={{32,0},{64,32},{96,64},{128,96},{160,128},{192,160},{224,192},{256... | collective-permute-start | bytes 399368 | tf_op jit(solution)/shard_map/ppermute | solution.py:15
  19.4 4.5 %collective-permute-start = (bf16[260,1,8,32]{0,3,2,1:T(8,128)(2,1)S(1)}, bf16[260,1,8,32]{0,3,2,1:T(8,128)(2,1)S(1)}, u32[]{:S(2)}, u32[]{:S(2)}) collective-permute-start(bf16[260,1,8,32]{0,3,2,1:T(8,128)(2,1)S(1)} %get-tuple-element.6), channel_id=1, source_target_pairs={{0,32},{32,64},{64,96},{96,128},{128,160},{160,192},{192,224},{224... | collective-permute-start | bytes 399368 | tf_op jit(solution)/shard_map/ppermute | solution.py:12
  24.1 6.9 %collective-permute-start.3 = (bf16[260,6,1,32]{0,3,2,1:T(8,128)(2,1)S(1)}, bf16[260,6,1,32]{0,3,2,1:T(8,128)(2,1)S(1)}, u32[]{:S(2)}, u32[]{:S(2)}) collective-permute-start(bf16[260,6,1,32]{0,3,2,1:T(8,128)(2,1)S(1)} %get-tuple-element.5), channel_id=1, source_target_pairs={{1,0},{2,1},{3,2},{4,3},{5,4},{6,5},{7,6},{8,7},{9,8},{10,9},{11,1... | collective-permute-start | bytes 299528 | tf_op jit(solution)/shard_map/ppermute | solution.py:15
  25.4 7.3 %collective-permute-start.2 = (bf16[260,6,1,32]{0,3,2,1:T(8,128)(2,1)S(1)}, bf16[260,6,1,32]{0,3,2,1:T(8,128)(2,1)}, u32[]{:S(2)}, u32[]{:S(2)}) collective-permute-start(bf16[260,6,1,32]{0,3,2,1:T(8,128)(2,1)S(1)} %get-tuple-element.4), channel_id=1, source_target_pairs={{0,1},{1,2},{2,3},{3,4},{4,5},{5,6},{6,7},{7,8},{8,9},{9,10},{10,1... | collective-permute-start | bytes 299528 | tf_op jit(solution)/shard_map/ppermute | solution.py:12
  31.0 0.7 copy-start.7
  37.3 4.1 %copy-start.1 = (bf16[260,6,10,32]{3,0,2,1:T(8,128)(2,1)S(1)}, bf16[260,6,10,32]{3,0,2,1:T(8,128)(2,1)}, u32[]{:S(2)}) copy-start(bf16[260,6,10,32]{3,0,2,1:T(8,128)(2,1)} %copy.132) | copy-start | bytes 2995204
  46.9 0.7 copy-start.11
  47.6 2.5 copy-start.6
  47.6 2.7 copy-start.3
  50.3 1.0 copy-start.8
  53.8 23.3 %copy-start.5 = (bf16[260,6,9,32]{0,3,2,1:T(8,128)(2,1)}, bf16[260,6,9,32]{0,3,2,1:T(8,128)(2,1)S(1)}, u32[]{:S(2)}) copy-start(bf16[260,6,9,32]{0,3,2,1:T(8,128)(2,1)S(1)} %get-tuple-element.2) | copy-start | bytes 2695684
  55.1 3.0 copy-start.10
  78.3 1.2 copy-start.4
Sparse Core Ops, SparseCore 0:
  79.7 284.1 all-reduce.2
where the time goes:
time: 374 us
  waiting for transfers between devices  176 us (47%)
  blocking collectives  107 us (29%)
  matrix products  33.1 us (9%)
  local copies, waits for them, and re-layouts  20.1 us (5%)
  starting transfers between devices  16.7 us (4%)
  between operations  14.4 us (4%)
  other arithmetic  6.36 us (2%)
    psum x1, waiting for transfers between devices, body(): grad_one, grad_two = lax.psum((grad_one, grad_two), ('ha', 'wa'))  173 us
    psum x1, blocking collectives, body(): grad_one, grad_two = lax.psum((grad_one, grad_two), ('ha', 'wa'))  107 us
    dot_general x54, matrix products, kernel_terms(): jnp.einsum('cp,op->co', window, flat_out, preferred_element_type=jnp.floa...  30.6 us
    ppermute x2, starting transfers between devices, padded_2(): lax.ppermute(lax.slice_in_dim(block, 0, width, axis=dim), axis, backward)  10.1 us
    unnamed x28, local copies, waits for them, and re-layouts  9.16 us
  transfers between devices with their start and end apart: 5, of which 4 were waited for; matrix products, arithmetic and copies ran while one was open for 2% of the time, Pallas kernels for 0%

commit v1 on v0

v1 whole, which is shorter than its diff:
```python
import functools

import jax
import jax.numpy as jnp
from jax import lax
from jax.experimental import pallas as pl
from jax.experimental.pallas import tpu as pltpu
from jax.sharding import PartitionSpec as P

MESH = pl.DeviceIdType.MESH
F32 = jnp.float32
BF16 = jnp.bfloat16
NY, NZ, NX = 8, 8, 4
TAPS = 28
GROUPS = 7
SIDES = [(a, b) for a in (-1, 0, 1) for b in (-1, 0, 1) if (a, b) != (0, 0)]
X_STEPS = (1, 3, 2)
RING = (1, 7, 2, 6, 3, 5, 4)


def span(side, size):
    if side == 0:
        return slice(0, size), slice(1, size + 1)
    if side == 1:
        return slice(size - 1, size), slice(0, 1)
    return slice(0, 1), slice(size + 1, size + 2)


def kernel(
    vol_ref, hid_ref, go_ref, w_ref, out_ref,
    ext, vols, hid, w, act_t, part, core_rx, x_tx, x_rx, y_tx, y_rx, y_own, z_all,
    load_sem, halo_ss, halo_rs, core_ss, core_rs, x_ss, x_rs, y_ss, y_rs, z_ss, z_rs,
    yg_ss, yg_rs, xg_ss, xg_rs, cg_ss, cg_rs,
):
    ha = lax.axis_index("ha")
    wa = lax.axis_index("wa")
    ys, core = ha // 2, ha % 2
    zs, xs = wa // 4, wa % 4
    n_ha, n_wa = 2 * NY, NX * NZ

    def dev(y, c, z, x):
        return (y * 2 + c, z * NX + x)

    def near(side):
        return ((ha + side[0] + n_ha) % n_ha, (wa + side[1] + n_wa) % n_wa)

    other = dev(ys, 1 - core, zs, xs)
    x_peer = [dev(ys, core, zs, (xs + i) % NX) for i in X_STEPS]
    y_peer = [dev((ys + i) % NY, core, zs, xs) for i in RING]
    z_peer = [dev(ys, core, (zs + i) % NZ, xs) for i in RING]

    loads = [
        pltpu.make_async_copy(hid_ref, hid, load_sem.at[0]),
        pltpu.make_async_copy(go_ref, ext.at[1:5, 1:9], load_sem.at[1]),
        pltpu.make_async_copy(vol_ref, vols.at[4], load_sem.at[2]),
        pltpu.make_async_copy(w_ref, w, load_sem.at[3]),
    ]
    for c in loads:
        c.start()

    barrier = pltpu.get_barrier_semaphore()
    greet = [near(s) for s in SIDES] + x_peer + y_peer + z_peer
    for d in greet:
        pl.semaphore_signal(barrier, inc=1, device_id=d, device_id_type=MESH)

    copies = []

    def send(src, dst, ss, rs, device):
        c = pltpu.make_async_remote_copy(
            src_ref=src, dst_ref=dst, send_sem=ss, recv_sem=rs,
            device_id=device, device_id_type=MESH,
        )
        return c

    halo = []
    for n, side in enumerate(SIDES):
        (sh, dh), (sw, dw) = span(side[0], 4), span(side[1], 8)
        slot = (1 - side[0]) * 3 + (1 - side[1])
        halo.append(send(go_ref.at[sh, sw], ext.at[dh, dw], halo_ss.at[n], halo_rs.at[n], near(side)))
        halo.append(send(vol_ref, vols.at[slot], halo_ss.at[8 + n], halo_rs.at[8 + n], near(side)))

    pl.semaphore_wait(barrier, len(greet))
    for c in halo[0::2] + halo[1::2]:
        c.start()

    loads[0].wait()
    depth = lax.broadcasted_iota(jnp.int32, (1024, 128), 0) % 32
    act = jnp.maximum(hid[...], 0).astype(F32).reshape(1024, 128)
    act_t[128:256, :] = act.astype(BF16).T
    lower = jnp.where(depth == 0, 0.0, pltpu.roll(act, 1, 0))
    act_t[0:128, :] = lower.astype(BF16).T
    upper = jnp.where(depth == 31, 0.0, pltpu.roll(act, 1023, 0))
    act_t[256:384, :] = upper.astype(BF16).T

    for c in loads[1:]:
        c.wait()
    for c in halo:
        c.wait()

    for edge, rows in ((0, slice(0, 1)), (n_ha - 1, slice(5, 6))):
        @pl.when(ha == edge)
        def _(rows=rows):
            ext[rows] = jnp.zeros((1, 10, 32, 128), BF16)
            first = 0 if rows.start == 0 else 6
            vols[first : first + 3] = jnp.zeros((3, 32, 256), BF16)

    for edge, cols in ((0, slice(0, 1)), (n_wa - 1, slice(9, 10))):
        @pl.when(wa == edge)
        def _(cols=cols):
            ext[:, cols] = jnp.zeros((6, 1, 32, 128), BF16)
            first = 0 if cols.start == 0 else 2
            for n in (first, first + 3, first + 6):
                vols[n] = jnp.zeros((32, 256), BF16)

    def window(g):
        kh, kw = g // 3, g % 3
        return ext[2 - kh : 6 - kh, 2 - kw : 10 - kw].reshape(1024, 128)

    def taps_of(g):
        return slice(3 * g, 3 * g + 3) if g < 9 else slice(27, 28)

    their_half = pl.ds(pl.multiple_of((1 - core) * 64, 64), 64)
    own_half = pl.ds(pl.multiple_of(core * 64, 64), 64)
    own_in_half = pl.ds(pl.multiple_of(xs * 16, 16), 16)
    own_rows = pl.ds(pl.multiple_of(core * 64 + xs * 16, 16), 16)

    def rows_of(c, x):
        return pl.ds(pl.multiple_of(c * 64 + x * 16, 16), 16)

    core_copies = []

    def core_send(g):
        t = taps_of(g)
        c = send(part.at[t, their_half], core_rx.at[t], core_ss.at[g], core_rs.at[g], other)
        c.start()
        core_copies.append(c)

    x_copies = []

    def x_send(g):
        t = taps_of(g)
        core_copies[g].wait_recv()
        x_tx[t] = (part[t, own_half] + core_rx[t]).astype(BF16)
        row = []
        for i, step in enumerate(X_STEPS):
            rows = pl.ds(pl.multiple_of((xs + step) % NX * 16, 16), 16)
            c = send(x_tx.at[t, rows], x_rx.at[i, t], x_ss.at[g, i], x_rs.at[g, i], x_peer[i])
            c.start()
            row.append(c)
        x_copies.append(row)

    for pair in ((0, 1), (2, 3), (4, 5), (6, 7), (8,)):
        right = jnp.concatenate([window(g) for g in pair], axis=1)
        terms = jnp.dot(act_t[...], right, preferred_element_type=F32)
        for n, g in enumerate(pair):
            part[taps_of(g)] = terms[:, 128 * n : 128 * n + 128].reshape(3, 128, 128)
            core_send(g)
        for g in pair:
            if g >= 2:
                x_send(g - 2)

    def column(n):
        return jnp.concatenate(
            [vols[n, 24:32], vols[3 + n], vols[6 + n, 0:8]], axis=0
        ).astype(F32)

    left, centre, right = column(0), column(1), column(2)
    lane = lax.broadcasted_iota(jnp.int32, (48, 256), 1)
    by_w = [
        jnp.where(lane < 32, pltpu.roll(left, 32, 1), pltpu.roll(centre, 32, 1)),
        centre,
        jnp.where(lane >= 224, pltpu.roll(right, 224, 1), pltpu.roll(centre, 224, 1)),
    ]
    blocks = []
    for field in by_w:
        blocks.append(jnp.where(lane % 32 == 0, 0.0, pltpu.roll(field, 1, 1)))
        blocks.append(field)
        blocks.append(jnp.where(lane % 32 == 31, 0.0, pltpu.roll(field, 255, 1)))
    fields = jnp.concatenate(blocks, axis=0).astype(BF16)

    one = [[jnp.zeros((8, 128), F32) for _ in range(3)] for _ in range(9)]
    depth_row = lax.broadcasted_iota(jnp.int32, (256, 128), 0) % 32
    weights = jnp.concatenate([w[g] for g in range(9)], axis=1)
    for h in range(4):
        cells = jnp.concatenate(
            [
                ext[h + 2 - g // 3, 2 - g % 3 : 10 - g % 3].reshape(256, 128)
                for g in range(9)
            ],
            axis=1,
        )
        pulled = lax.dot_general(
            cells, weights, (((1,), (1,)), ((), ())), preferred_element_type=F32
        )
        grad = (
            jnp.where(depth_row == 31, 0.0, pltpu.roll(pulled[:, 0:128], 255, 0))
            + pulled[:, 128:256]
            + jnp.where(depth_row == 0, 0.0, pltpu.roll(pulled[:, 256:384], 1, 0))
        )
        mask = hid[h].reshape(256, 128).astype(F32) > 0
        grad_hidden = jnp.where(mask, grad, 0.0).astype(BF16)
        terms = jnp.dot(fields, grad_hidden, preferred_element_type=F32)
        for b in range(9):
            for kh in range(3):
                first = b * 48 + (h + kh) * 8
                one[b][kh] = one[b][kh] + terms[first : first + 8]
        if h == 1:
            x_send(7)
            x_send(8)
    part[27] = jnp.zeros((128, 128), F32)
    for b in range(9):
        for kh in range(3):
            first = (b * 3 + kh) * 4
            part[27, first : first + 4, :] = one[b][kh][0:4]
    core_send(9)

    def group(j):
        return slice(4 * j, 4 * j + 4)

    def y_copy(j):
        return send(
            y_tx.at[j], y_rx.at[ys], y_ss.at[j], y_rs.at[ys], dev(j, core, zs, xs)
        )

    y_rx[ys] = jnp.zeros((4, 16, 128), BF16)
    waited = 0
    for j in range(GROUPS):
        if j == GROUPS - 1:
            x_send(9)
        need = 10 if j == GROUPS - 1 else (4 * j + 3) // 3 + 1
        while waited < need:
            for c in x_copies[waited]:
                c.wait_recv()
            waited += 1
        t = group(j)
        total = part[t, own_rows] + core_rx[t, own_in_half]
        for i in range(3):
            total = total + x_rx[i, t].astype(F32)

        @pl.when(ys == j)
        def _(total=total):
            y_own[...] = total

        @pl.when(ys != j)
        def _(total=total, j=j):
            y_tx[j] = total.astype(BF16)
            y_copy(j).start()

    own_group = pl.ds(ys * 4, 4)

    def z_copy(i):
        return send(z_all.at[zs], z_all.at[zs], z_ss.at[i], z_rs.at[i], z_peer[i])

    def yg_copy(i):
        place = out_ref.at[own_group, own_rows]
        return send(place, place, yg_ss.at[i], yg_rs.at[ys], y_peer[i])

    @pl.when(ys < GROUPS)
    def _():
        for s in range(NY):
            @pl.when(ys != s)
            def _(s=s):
                send(y_tx.at[0], y_rx.at[s], y_ss.at[0], y_rs.at[s], other).wait_recv()

        total = y_own[...]
        for s in range(NY):
            total = total + y_rx[s].astype(F32)
        z_all[zs] = total
        for i in range(7):
            z_copy(i).start()
        for i in range(7):
            z_copy(i).wait_recv()
        total = z_all[0]
        for s in range(1, NZ):
            total = total + z_all[s]
        out_ref[own_group, own_rows] = total.astype(BF16)
        for i in range(7):
            yg_copy(i).start()

    def xg_copy(j, i):
        place = out_ref.at[group(j), own_rows]
        return send(place, place, xg_ss.at[j, i], xg_rs.at[j, i], x_peer[i])

    def cg_copy(j, i):
        x = xs if i == 3 else (xs + NX - X_STEPS[i]) % NX
        place = out_ref.at[group(j), rows_of(core, x)]
        return send(place, place, cg_ss.at[j, i], cg_rs.at[j, i], other)

    for j in range(GROUPS):
        @pl.when(ys != j)
        def _(j=j):
            place = out_ref.at[group(j), own_rows]
            send(place, place, yg_ss.at[0], yg_rs.at[j], other).wait_recv()

        for i in range(3):
            xg_copy(j, i).start()
        cg_copy(j, 3).start()
    for j in range(GROUPS):
        for i in range(3):
            xg_copy(j, i).wait_recv()
            cg_copy(j, i).start()
    for j in range(GROUPS):
        for i in range(4):
            cg_copy(j, i).wait_recv()

    for c in core_copies:
        c.wait_send()
    for row in x_copies:
        for c in row:
            c.wait_send()
    for j in range(GROUPS):
        @pl.when(ys != j)
        def _(j=j):
            y_copy(j).wait_send()

    @pl.when(ys < GROUPS)
    def _():
        for i in range(7):
            z_copy(i).wait_send()
        for i in range(7):
            yg_copy(i).wait_send()

    for j in range(GROUPS):
        for i in range(3):
            xg_copy(j, i).wait_send()
        for i in range(4):
            cg_copy(j, i).wait_send()


def body(volume, hidden_pre, grad_out, weight_two):
    vol = jnp.transpose(volume, (1, 0, 2, 3)).reshape(4, 4, 256)
    vol = jnp.pad(vol, ((0, 0), (0, 4), (0, 0))).reshape(32, 256)
    hid = jnp.transpose(hidden_pre, (1, 2, 3, 0))
    grad = jnp.transpose(grad_out, (1, 2, 3, 0))
    weights = weight_two.reshape(9, 384, 128)
    dma = pltpu.SemaphoreType.DMA
    out = pl.pallas_call(
        kernel,
        out_shape=jax.ShapeDtypeStruct((TAPS, 128, 128), BF16),
        in_specs=[pl.BlockSpec(memory_space=pl.ANY)] * 4,
        out_specs=pl.BlockSpec(memory_space=pltpu.VMEM),
        scratch_shapes=[
            pltpu.VMEM((6, 10, 32, 128), BF16),
            pltpu.VMEM((9, 32, 256), BF16),
            pltpu.VMEM((4, 8, 32, 128), BF16),
            pltpu.VMEM((9, 384, 128), BF16),
            pltpu.VMEM((384, 1024), BF16),
            pltpu.VMEM((TAPS, 128, 128), F32),
            pltpu.VMEM((TAPS, 64, 128), F32),
            pltpu.VMEM((TAPS, 64, 128), BF16),
            pltpu.VMEM((3, TAPS, 16, 128), BF16),
            pltpu.VMEM((GROUPS, 4, 16, 128), BF16),
            pltpu.VMEM((NY, 4, 16, 128), BF16),
            pltpu.VMEM((4, 16, 128), F32),
            pltpu.VMEM((NZ, 4, 16, 128), F32),
            dma((4,)), dma((16,)), dma((16,)), dma((10,)), dma((10,)), dma((10, 3)), dma((10, 3)),
            dma((GROUPS,)), dma((NY,)), dma((7,)), dma((7,)), dma((7,)), dma((NY,)),
            dma((GROUPS, 3)), dma((GROUPS, 3)), dma((GROUPS, 4)), dma((GROUPS, 4)),
        ],
        compiler_params=pltpu.CompilerParams(
            collective_id=0, has_side_effects=True, vmem_limit_bytes=40 * 1024 * 1024
        ),
        name="conv_backward",
    )(vol, hid, grad, weights)
    one = out[27, :108].reshape(3, 3, 3, 4, 128).astype(F32)
    grad_one = jnp.transpose(one, (2, 0, 1, 3, 4))
    grad_two = out[:27].reshape(3, 3, 3, 128, 128).astype(F32)
    return (grad_one, grad_two)


def solution(mesh):
    in_specs = (
        P(None, "ha", "wa", None),
        P(None, "ha", "wa", None),
        P(None, "ha", "wa", None),
        P(),
    )
    return jax.shard_map(body, mesh=mesh, in_specs=in_specs, out_specs=(P(), P()), check_vma=False)
```

time: 374 us -> 65.3 us (0.17)
  waiting for transfers between devices: 176 us -> 0 us
  blocking collectives: 107 us -> 0 us
  Pallas kernels: 0 us -> 58.2 us
  matrix products: 33.1 us -> 0 us
  starting transfers between devices: 16.7 us -> 0 us
  local copies, waits for them, and re-layouts: 20.1 us -> 4.67 us
  between operations: 14.4 us -> 0.69 us
  other arithmetic: 6.36 us -> 1.41 us
    psum x1 -> x0, waiting for transfers between devices: 173 us -> none  [body(): grad_one, grad_two = lax.psum((grad_one, grad_two), ('ha', 'wa'))]
    psum x1 -> x0, blocking collectives: 107 us -> none  [body(): grad_one, grad_two = lax.psum((grad_one, grad_two), ('ha', 'wa'))]
    pallas_call x0 -> x1, Pallas kernels: none -> 58.2 us  [body(): pl.pallas_call(kernel, out_shape=jax.ShapeDtypeStruct((TAPS, 128, 128), B...]
    dot_general x54 -> x0, matrix products: 30.6 us -> none  [kernel_terms(): jnp.einsum('cp,op->co', window, flat_out, preferred_element_type=jnp.floa...]
    ppermute x4 -> x0, starting transfers between devices: 16.6 us -> none  [the longest x2 10.1 us: padded_2(): lax.ppermute(lax.slice_in_dim(block, 0, width, axis=dim), axis, backward)]
    unnamed x28 -> x7, local copies, waits for them, and re-layouts: 9.16 us -> 3.69 us
    broadcast_in_dim x2 -> x0, local copies, waits for them, and re-layouts: 4.25 us -> none  [body(): grad_pad[None]]
    concatenate x2 -> x0, other arithmetic: 3.86 us -> none  [padded_2(): block = jnp.concatenate([low, block, high], axis=dim)]
  transfers between devices with their start and end apart: 5 -> 0, of which waited for: 4 -> 0; matrix products, arithmetic and copies ran while one was open for 2% -> 0% of each run, Pallas kernels for 0% -> 0%
where the time goes in v1:
time: 65.3 us; the launch traced here: 65 us
  Pallas kernels  58.2 us (89%)
  local copies, waits for them, and re-layouts  4.67 us (7%)
  other arithmetic  1.41 us (2%)
  between operations  0.69 us (1%)
    pallas_call x1, Pallas kernels, body(): pl.pallas_call(kernel, out_shape=jax.ShapeDtypeStruct((TAPS, 128, 128), B...  58.2 us
    unnamed x7, local copies, waits for them, and re-layouts  3.69 us
    convert_element_type x1, other arithmetic, body(): grad_two = out[:27].reshape(3, 3, 3, 128, 128).astype(F32)  1.41 us

profile of v1, /device:TPU:1, one launch (start us, length us, event | category | flops | bytes accessed | tf_op | source)
XLA Modules:
  0.0 65.0 jit_solution(2197515616990362966)
XLA Ops:
  0.6 0.9 %reshape.18 = bf16[4,4,256]{2,0,1:T(4,128)(2,1)S(1)} reshape(bf16[4,4,8,32]{3,2,0,1:T(8,128)(2,1)} %bitcast.18) | data formatting | bytes 16384 | tf_op jit(solution)/shard_map/reshape | solution.py:331
  1.5 0.0 copy-start
  1.5 1.2 %copy-done = bf16[3,3,3,128,128]{4,3,2,1,0:T(8,128)(2,1)S(1)} copy-done((bf16[3,3,3,128,128]{4,3,2,1,0:T(8,128)(2,1)S(1)}, bf16[3,3,3,128,128]{4,3,2,1,0:T(8,128)(2,1)}, u32[]{:S(2)}) %copy-start) | copy-done | bytes 884760
  2.7 0.0 copy-start.1
  2.7 0.9 %copy-done.1 = bf16[128,4,8,32]{0,3,2,1:T(8,128)(2,1)S(1)} copy-done((bf16[128,4,8,32]{0,3,2,1:T(8,128)(2,1)S(1)}, bf16[128,4,8,32]{0,3,2,1:T(8,128)(2,1)}, u32[]{:S(2)}) %copy-start.1) | copy-done | bytes 262168
  3.6 0.0 copy-start.2
  3.6 0.9 %copy-done.2 = bf16[128,4,8,32]{0,3,2,1:T(8,128)(2,1)S(1)} copy-done((bf16[128,4,8,32]{0,3,2,1:T(8,128)(2,1)S(1)}, bf16[128,4,8,32]{0,3,2,1:T(8,128)(2,1)}, u32[]{:S(2)}) %copy-start.2) | copy-done | bytes 262168
  4.6 58.2 %conv_backward.1 = bf16[28,128,128]{2,1,0:T(8,128)(2,1)S(1)} custom-call(bf16[32,256]{1,0:T(8,128)(2,1)S(1)} %pad_bitcast_fusion.vol_ref, bf16[4,8,32,128]{3,2,1,0:T(8,128)(2,1)S(1)} %bitcast.14, bf16[4,8,32,128]{3,2,1,0:T(8,128)(2,1)S(1)} %bitcast.15, bf16[9,384,128]{2,1,0:T(8,128)(2,1)S(1)} %bitcast.13), custom_call_target="tpu_custom_call" | custom-call | tf_op jit(solution)/shard_map/conv_backward/pallas_call | solution.py:337
  62.8 0.1 slice.7
  63.0 0.6 copy.9
  63.6 1.4 %convert.3 = f32[3,3,3,128,128]{4,3,2,1,0:T(8,128)} convert(bf16[3,3,3,128,128]{4,3,2,1,0:T(8,128)(2,1)S(1)} %bitcast.16) | non-fusion elementwise | flops 442368 | bytes 2654208 | tf_op jit(solution)/shard_map/convert_element_type | solution.py:367
  (4 shorter events, 0.0 us)
Async XLA Ops:
  1.5 1.2 %copy-start = (bf16[3,3,3,128,128]{4,3,2,1,0:T(8,128)(2,1)S(1)}, bf16[3,3,3,128,128]{4,3,2,1,0:T(8,128)(2,1)}, u32[]{:S(2)}) copy-start(bf16[3,3,3,128,128]{4,3,2,1,0:T(8,128)(2,1)} %param.7) | copy-start | bytes 2654212
  2.7 0.9 %copy-start.1 = (bf16[128,4,8,32]{0,3,2,1:T(8,128)(2,1)S(1)}, bf16[128,4,8,32]{0,3,2,1:T(8,128)(2,1)}, u32[]{:S(2)}) copy-start(bf16[128,4,8,32]{0,3,2,1:T(8,128)(2,1)} %param.5) | copy-start | bytes 786436
  3.6 0.9 %copy-start.2 = (bf16[128,4,8,32]{0,3,2,1:T(8,128)(2,1)S(1)}, bf16[128,4,8,32]{0,3,2,1:T(8,128)(2,1)}, u32[]{:S(2)}) copy-start(bf16[128,4,8,32]{0,3,2,1:T(8,128)(2,1)} %param.6) | copy-start | bytes 786436

commit v2 on v1

v2 whole, which is shorter than its diff:
```python
import jax
import jax.numpy as jnp
from jax import lax
from jax.experimental import pallas as pl
from jax.experimental.pallas import tpu as pltpu
from jax.sharding import PartitionSpec as P

MESH = pl.DeviceIdType.MESH
F32 = jnp.float32
BF16 = jnp.bfloat16
NY, NZ, NX = 8, 8, 4
TAPS = 28
SIDES = [(a, b) for a in (-1, 0, 1) for b in (-1, 0, 1) if (a, b) != (0, 0)]
X_STEPS = (2, 1, 3)
RING = (1, 7, 2, 6, 3, 5, 4)
FAR_FIRST = (6, 5, 4, 3, 2, 1, 0)
LIVE = (8, 6)
SUM = F32
ONE_STEPS = ((1, 2), (0, 2), (1, 1), (1, 3), (0, 1), (0, 3), (1, 0))


def span(side, size):
    if side == 0:
        return slice(0, size), slice(1, size + 1)
    if side == 1:
        return slice(size - 1, size), slice(0, 1)
    return slice(0, 1), slice(size + 1, size + 2)


def kernel(
    vol_ref, hid_ref, go_ref, w_ref, out_ref,
    ext, vols, vol_raw, vol_rows, vol_flat, hid, w, act_t, part, core_rx, x_tx, x_rx,
    one_tx, one_rx, first_tx, first_rx, first_sum, second, stage,
    load_sem, halo_ss, halo_rs, core_ss, core_rs, x_ss, x_rs, o_ss, o_rs, f_ss, f_rs, s_ss, s_rs,
    g_ss, g_rs, xg_ss, xg_rs, cg_ss, cg_rs,
):
    ha = lax.axis_index("ha")
    wa = lax.axis_index("wa")
    ys, core = ha // 2, ha % 2
    zs, xs = wa // 4, wa % 4
    n_ha, n_wa = 2 * NY, NX * NZ

    def dev(y, c, z, x):
        return (y * 2 + c, z * NX + x)

    def near(side):
        return ((ha + side[0] + n_ha) % n_ha, (wa + side[1] + n_wa) % n_wa)

    other = dev(ys, 1 - core, zs, xs)
    x_peer = [dev(ys, core, zs, (xs + i) % NX) for i in X_STEPS]
    cross_peer = [dev(ys, 1 - core, zs, (xs + i) % NX) for i in X_STEPS]
    y_peer = [dev((ys + i) % NY, core, zs, xs) for i in RING]
    z_peer = [dev(ys, core, (zs + i) % NZ, xs) for i in RING]

    loads = [
        pltpu.make_async_copy(vol_ref, vol_raw, load_sem.at[0]),
        pltpu.make_async_copy(hid_ref, hid, load_sem.at[1]),
        pltpu.make_async_copy(go_ref, ext.at[1:5, 1:9], load_sem.at[2]),
        pltpu.make_async_copy(w_ref, w, load_sem.at[3]),
    ]
    for c in loads:
        c.start()

    barrier = pltpu.get_barrier_semaphore()
    greet = [near(s) for s in SIDES] + x_peer + cross_peer + y_peer + z_peer
    for d in greet:
        pl.semaphore_signal(barrier, inc=1, device_id=d, device_id_type=MESH)

    def send(src, dst, ss, rs, device):
        c = pltpu.make_async_remote_copy(
            src_ref=src, dst_ref=dst, send_sem=ss, recv_sem=rs,
            device_id=device, device_id_type=MESH,
        )
        return c

    halo, vol_halo = [], []
    for n, side in enumerate(SIDES):
        (sh, dh), (sw, dw) = span(side[0], 4), span(side[1], 8)
        slot = (1 - side[0]) * 3 + (1 - side[1])
        halo.append(send(go_ref.at[sh, sw], ext.at[dh, dw], halo_ss.at[n], halo_rs.at[n], near(side)))
        vol_halo.append(
            send(vols.at[4], vols.at[slot], halo_ss.at[8 + n], halo_rs.at[8 + n], near(side))
        )

    pl.semaphore_wait(barrier, len(greet))
    for c in halo:
        c.start()

    loads[0].wait()
    vol_rows[...] = jnp.zeros((128, 128), F32)
    vol_rows[:, 0:32] = vol_raw[...].astype(F32).reshape(128, 32)
    halves = []
    for half in range(2):
        lanes = jnp.zeros((16, 128), F32)
        for n in range(4):
            row = vol_rows[pl.ds(half * 4 + n, 16, stride=8), :]
            lanes = lanes + (pltpu.roll(row, 32 * n, 1) if n else row)
        halves.append(lanes)
    vol_flat[...] = jnp.zeros((32, 256), F32)
    for n in range(2):
        for c in range(4):
            for h in range(4):
                vol_flat[h * 8 + c : h * 8 + c + 1, 128 * n : 128 * n + 128] = halves[n][
                    c * 4 + h : c * 4 + h + 1
                ]
    vols[4] = vol_flat[...].astype(BF16)

    for c in vol_halo:
        c.start()

    loads[1].wait()
    depth = lax.broadcasted_iota(jnp.int32, (1024, 128), 0) % 32
    act = jnp.maximum(hid[...], 0).astype(F32).reshape(1024, 128)
    act_t[128:256, :] = act.astype(BF16).T
    lower = jnp.where(depth == 0, 0.0, pltpu.roll(act, 1, 0))
    act_t[0:128, :] = lower.astype(BF16).T
    upper = jnp.where(depth == 31, 0.0, pltpu.roll(act, 1023, 0))
    act_t[256:384, :] = upper.astype(BF16).T
    loads[2].wait()

    def window(g):
        kh, kw = g // 3, g % 3
        return ext[2 - kh : 6 - kh, 2 - kw : 10 - kw].reshape(1024, 128)

    def taps_of(g):
        return slice(3 * g, 3 * g + 3)

    their_half = pl.ds(pl.multiple_of((1 - core) * 64, 64), 64)
    own_half = pl.ds(pl.multiple_of(core * 64, 64), 64)
    own_in_half = pl.ds(pl.multiple_of(xs * 16, 16), 16)
    own_rows = pl.ds(pl.multiple_of(core * 64 + xs * 16, 16), 16)

    core_copies, x_copies = {}, {}

    def core_send(g):
        t = taps_of(g)
        c = send(part.at[t, their_half], core_rx.at[t], core_ss.at[g], core_rs.at[g], other)
        c.start()
        core_copies[g] = c

    def x_send(g):
        t = taps_of(g)
        core_copies[g].wait_recv()
        x_tx[t] = (part[t, own_half] + core_rx[t]).astype(BF16)
        x_copies[g] = []
        for i, step in enumerate(X_STEPS):
            rows = pl.ds(pl.multiple_of((xs + step) % NX * 16, 16), 16)
            c = send(x_tx.at[t, rows], x_rx.at[i, t], x_ss.at[g, i], x_rs.at[g, i], x_peer[i])
            c.start()
            x_copies[g].append(c)

    def grad_two(pair):
        right = jnp.concatenate([window(g) for g in pair], axis=1)
        terms = jnp.dot(act_t[...], right, preferred_element_type=F32)
        for n, g in enumerate(pair):
            part[taps_of(g)] = terms[:, 128 * n : 128 * n + 128].reshape(3, 128, 128)
            core_send(g)

    grad_two((4,))

    for c in halo:
        c.wait_recv()
    for edge, row in ((0, 0), (n_ha - 1, 5)):
        @pl.when(ha == edge)
        def _(row=row):
            ext[row : row + 1] = jnp.zeros((1, 10, 32, 128), BF16)

    for edge, col in ((0, 0), (n_wa - 1, 9)):
        @pl.when(wa == edge)
        def _(col=col):
            ext[:, col : col + 1] = jnp.zeros((6, 1, 32, 128), BF16)

    grad_two((0, 1))
    grad_two((2, 3))
    x_send(4)
    grad_two((5, 6))
    x_send(0)
    x_send(1)
    grad_two((7, 8))
    x_send(2)
    x_send(3)

    for c in vol_halo:
        c.wait_recv()
    for edge, first in ((0, 0), (n_ha - 1, 6)):
        @pl.when(ha == edge)
        def _(first=first):
            vols[first : first + 3] = jnp.zeros((3, 32, 256), BF16)

    for edge, first in ((0, 0), (n_wa - 1, 2)):
        @pl.when(wa == edge)
        def _(first=first):
            for n in (first, first + 3, first + 6):
                vols[n] = jnp.zeros((32, 256), BF16)

    def column(n):
        rows = [vols[n].astype(F32)[24:32], vols[3 + n].astype(F32), vols[6 + n].astype(F32)[0:8]]
        return jnp.concatenate(rows, axis=0)

    left, centre, right = column(0), column(1), column(2)
    lane = lax.broadcasted_iota(jnp.int32, (48, 256), 1)
    by_w = [
        jnp.where(lane < 32, pltpu.roll(left, 32, 1), pltpu.roll(centre, 32, 1)),
        centre,
        jnp.where(lane >= 224, pltpu.roll(right, 224, 1), pltpu.roll(centre, 224, 1)),
    ]
    blocks = []
    for field in by_w:
        blocks.append(jnp.where(lane % 32 == 0, 0.0, pltpu.roll(field, 1, 1)))
        blocks.append(field)
        blocks.append(jnp.where(lane % 32 == 31, 0.0, pltpu.roll(field, 255, 1)))
    fields = jnp.concatenate(blocks, axis=0).astype(BF16)

    loads[3].wait()
    one = [[jnp.zeros((8, 128), F32) for _ in range(3)] for _ in range(9)]
    depth_row = lax.broadcasted_iota(jnp.int32, (256, 128), 0) % 32
    weights = jnp.concatenate([w[g] for g in range(9)], axis=1)
    for h in range(4):
        cells = jnp.concatenate(
            [
                ext[h + 2 - g // 3, 2 - g % 3 : 10 - g % 3].reshape(256, 128)
                for g in range(9)
            ],
            axis=1,
        )
        pulled = lax.dot_general(
            cells, weights, (((1,), (1,)), ((), ())), preferred_element_type=F32
        )
        grad = (
            jnp.where(depth_row == 31, 0.0, pltpu.roll(pulled[:, 0:128], 255, 0))
            + pulled[:, 128:256]
            + jnp.where(depth_row == 0, 0.0, pltpu.roll(pulled[:, 256:384], 1, 0))
        )
        mask = hid[h].reshape(256, 128).astype(F32) > 0
        grad_hidden = jnp.where(mask, grad, 0.0).astype(BF16)
        terms = jnp.dot(fields, grad_hidden, preferred_element_type=F32)
        for b in range(9):
            for kh in range(3):
                first = b * 48 + (h + kh) * 8
                one[b][kh] = one[b][kh] + terms[first : first + 8]
        if h == 0:
            x_send(5)
            x_send(6)
        if h == 1:
            x_send(7)
            x_send(8)
    part[27] = jnp.zeros((128, 128), F32)
    for b in range(9):
        for kh in range(3):
            first = (kh * 9 + b) * 4
            part[27, first : first + 4, :] = one[b][kh][0:4]
    one_tx[...] = part[27].astype(BF16)
    one_copies = []
    for i, (c, step) in enumerate(ONE_STEPS):
        half = core if c == 0 else 1 - core
        rows = pl.ds(pl.multiple_of(half * 64 + (xs + step) % NX * 16, 16), 16)
        device = other if step == 0 else (cross_peer if c else x_peer)[X_STEPS.index(step)]
        one_copies.append(send(one_tx.at[rows], one_rx.at[i], o_ss.at[i], o_rs.at[i], device))
        one_copies[i].start()

    place = (ys, zs)
    peers = (y_peer, z_peer)

    def first_copy(k, j):
        target = dev(j, core, zs, xs) if k == 0 else dev(ys, core, j, xs)
        return send(
            first_tx.at[k, j], first_rx.at[k, place[k]],
            f_ss.at[k, j], f_rs.at[k, place[k]], target,
        )

    seen = set()

    def first_send(k, j):
        lo = 16 * k + 2 * j
        hi = min(lo + 2, 27)
        for g in range(lo // 3, (hi - 1) // 3 + 1):
            if g not in seen:
                seen.add(g)
                for c in x_copies[g]:
                    c.wait_recv()
        t = slice(lo, hi)
        total = part[t, own_rows] + core_rx[t, own_in_half]
        for i in range(3):
            total = total + x_rx[i, t].astype(F32)
        first_sum[t] = total
        if hi == 27:
            one_total = part[27, own_rows]
            for i in range(7):
                one_copies[i].wait_recv()
                one_total = one_total + one_rx[i].astype(F32)
            first_sum[27] = one_total
        first_tx[k, j] = first_sum[lo : lo + 2].astype(BF16)

        @pl.when(place[k] != j)
        def _():
            first_copy(k, j).start()

    def second_copy(k, i):
        at = second.at[k, place[1 - k]]
        return send(at, at, s_ss.at[k, i], s_rs.at[k, i], peers[1 - k][i])

    def second_send(k):
        for s in range(8):
            @pl.when(place[k] != s)
            def _(s=s):
                send(
                    first_tx.at[k, 0], first_rx.at[k, s], f_ss.at[k, 0], f_rs.at[k, s], other
                ).wait_recv()

        total = first_sum[pl.ds(16 * k + 2 * place[k], 2)]
        for s in range(8):
            total = total + jnp.where(place[k] == s, 0.0, first_rx[k, s].astype(F32))
        second[k, place[1 - k]] = total.astype(SUM)
        for i in FAR_FIRST:
            second_copy(k, i).start()

    def gather_copy(k, i):
        return send(
            stage.at[0, k, 0, 0], stage.at[0, k, 0, 1 + i], g_ss.at[k, i], g_rs.at[k, i], peers[k][i]
        )

    def finish(k):
        for i in range(7):
            second_copy(k, i).wait_recv()
        total = second[k, 0].astype(F32)
        for s in range(1, 8):
            total = total + second[k, s].astype(F32)
        stage[0, k, 0, 0] = total.astype(BF16)

    def gather(k):
        for i in FAR_FIRST:
            gather_copy(k, i).start()

    def xg_copy(k, i):
        return send(
            stage.at[0, k, 0], stage.at[0, k, 1 + i], xg_ss.at[k, i], xg_rs.at[k, i], x_peer[i]
        )

    def cg_copy(k, m):
        r = slice(1, 4) if m else slice(0, 1)
        return send(stage.at[0, k, r], stage.at[1, k, r], cg_ss.at[k, m], cg_rs.at[k, m], other)

    def spread(k):
        for i in range(7):
            gather_copy(k, i).wait_recv()
        for i in range(3):
            xg_copy(k, i).start()
        cg_copy(k, 0).start()

    def forward(k):
        for i in range(3):
            xg_copy(k, i).wait_recv()
        cg_copy(k, 1).start()

    def put(c, k, r):
        half = core if c == 0 else 1 - core
        x = xs if r == 0 else (xs + NX - X_STEPS[r - 1]) % NX
        rows = pl.ds(pl.multiple_of(half * 64 + x * 16, 16), 16)
        for s in range(8):
            j = place[k] if s == 0 else (place[k] + 8 - RING[s - 1]) % 8
            out_ref[pl.ds(16 * k + 2 * j, 2), rows] = stage[c, k, r, s]

    live = place[1] < LIVE[1]
    for j in range(LIVE[0]):
        first_send(0, j)
    for j in range(LIVE[1]):
        first_send(1, j)
    second_send(0)
    pl.when(live)(lambda: second_send(1))

    for c in halo + vol_halo:
        c.wait_send()
    for g in range(9):
        core_copies[g].wait_send()

    finish(0)
    gather(0)
    pl.when(live)(lambda: finish(1))

    @pl.when(place[1] >= LIVE[1])
    def _():
        stage[0, 1, 0, 0] = jnp.zeros((2, 16, 128), BF16)

    gather(1)
    for g in range(9):
        for c in x_copies[g]:
            c.wait_send()
    for c in one_copies:
        c.wait_send()
    spread(0)
    spread(1)

    for k in range(2):
        for j in range(LIVE[k]):
            @pl.when(place[k] != j)
            def _(k=k, j=j):
                first_copy(k, j).wait_send()

    def second_left(k):
        for i in range(7):
            second_copy(k, i).wait_send()

    second_left(0)
    pl.when(live)(lambda: second_left(1))
    for k in range(2):
        put(0, k, 0)
        for i in range(7):
            gather_copy(k, i).wait_send()
    forward(0)
    for r in range(1, 4):
        put(0, 0, r)
    cg_copy(0, 0).wait_recv()
    put(1, 0, 0)
    forward(1)
    for r in range(1, 4):
        put(0, 1, r)
    cg_copy(1, 0).wait_recv()
    put(1, 1, 0)
    for k in range(2):
        for i in range(3):
            xg_copy(k, i).wait_send()
        cg_copy(k, 0).wait_send()
    for k in range(2):
        cg_copy(k, 1).wait_recv()
        for r in range(1, 4):
            put(1, k, r)
        cg_copy(k, 1).wait_send()


def widen(sums_ref, one_ref, two_ref, sums, one, two, sem):
    ins = []
    for n in range(4):
        t = slice(7 * n, 7 * n + 7)
        ins.append(pltpu.make_async_copy(sums_ref.at[t], sums.at[t], sem.at[n]))
        ins[n].start()
    outs = []
    for n in range(4):
        ins[n].wait()
        t = slice(7 * n, min(7 * n + 7, 27))
        two[t] = sums[t].astype(F32)
        outs.append(pltpu.make_async_copy(two.at[t], two_ref.at[t], sem.at[4 + n]))
        outs[n].start()
    rows = sums[27].astype(F32)
    for n in range(27):
        one[n] = rows[4 * n : 4 * n + 4]
    outs.append(pltpu.make_async_copy(one, one_ref, sem.at[8]))
    outs[4].start()
    for c in outs:
        c.wait()


def body(volume, hidden_pre, grad_out, weight_two):
    hid = jnp.transpose(hidden_pre, (1, 2, 3, 0))
    grad = jnp.transpose(grad_out, (1, 2, 3, 0))
    weights = weight_two.reshape(9, 384, 128)
    dma = pltpu.SemaphoreType.DMA
    out = pl.pallas_call(
        kernel,
        out_shape=jax.ShapeDtypeStruct((32, 128, 128), BF16),
        in_specs=[pl.BlockSpec(memory_space=pltpu.HBM)] * 4,
        out_specs=pl.BlockSpec(memory_space=pltpu.VMEM),
        scratch_shapes=[
            pltpu.VMEM((6, 10, 32, 128), BF16),
            pltpu.VMEM((9, 32, 256), BF16),
            pltpu.VMEM((4, 4, 8, 32), BF16),
            pltpu.VMEM((128, 128), F32),
            pltpu.VMEM((32, 256), F32),
            pltpu.VMEM((4, 8, 32, 128), BF16),
            pltpu.VMEM((9, 384, 128), BF16),
            pltpu.VMEM((384, 1024), BF16),
            pltpu.VMEM((TAPS, 128, 128), F32),
            pltpu.VMEM((27, 64, 128), F32),
            pltpu.VMEM((27, 64, 128), BF16),
            pltpu.VMEM((3, 27, 16, 128), BF16),
            pltpu.VMEM((128, 128), BF16),
            pltpu.VMEM((7, 16, 128), BF16),
            pltpu.VMEM((2, 8, 2, 16, 128), BF16),
            pltpu.VMEM((2, 8, 2, 16, 128), BF16),
            pltpu.VMEM((TAPS, 16, 128), F32),
            pltpu.VMEM((2, 8, 2, 16, 128), SUM),
            pltpu.VMEM((2, 2, 4, 8, 2, 16, 128), BF16),
            dma((4,)), dma((16,)), dma((16,)), dma((9,)), dma((9,)), dma((9, 3)), dma((9, 3)),
            dma((7,)), dma((7,)), dma((2, 8)), dma((2, 8)), dma((2, 7)), dma((2, 7)), dma((2, 7)), dma((2, 7)),
            dma((2, 3)), dma((2, 3)), dma((2, 2)), dma((2, 2)),
        ],
        compiler_params=pltpu.CompilerParams(
            collective_id=0, has_side_effects=True, vmem_limit_bytes=60 * 1024 * 1024
        ),
        name="conv_backward",
    )(volume, hid, grad, weights)
    one, two = pl.pallas_call(
        widen,
        out_shape=(
            jax.ShapeDtypeStruct((27, 4, 128), F32),
            jax.ShapeDtypeStruct((27, 128, 128), F32),
        ),
        in_specs=[pl.BlockSpec(memory_space=pl.ANY)],
        out_specs=(pl.BlockSpec(memory_space=pl.ANY),) * 2,
        scratch_shapes=[
            pltpu.VMEM((TAPS, 128, 128), BF16),
            pltpu.VMEM((27, 4, 128), F32),
            pltpu.VMEM((27, 128, 128), F32),
            dma((9,)),
        ],
        compiler_params=pltpu.CompilerParams(vmem_limit_bytes=60 * 1024 * 1024),
        name="widen",
    )(out)
    return (one.reshape(3, 3, 3, 4, 128), two.reshape(3, 3, 3, 128, 128))


def solution(mesh):
    in_specs = (
        P(None, "ha", "wa", None),
        P(None, "ha", "wa", None),
        P(None, "ha", "wa", None),
        P(),
    )
    return jax.shard_map(body, mesh=mesh, in_specs=in_specs, out_specs=(P(), P()), check_vma=False)
```

time: 65.3 us -> 56.8 us (0.87)
  local copies, waits for them, and re-layouts: 4.67 us -> 0 us
  Pallas kernels: 58.2 us -> 56 us
  other arithmetic: 1.41 us -> 0 us
    unnamed x7 -> x0, local copies, waits for them, and re-layouts: 3.69 us -> none
    pallas_call x1 -> x2, Pallas kernels: 58.2 us -> 56 us  [the longest x1 53.8 us: body(): pl.pallas_call(kernel, out_shape=jax.ShapeDtypeStruct((32, 128, 128), BF1...]
    convert_element_type x1 -> x0, other arithmetic: 1.41 us -> none  [body(): grad_two = out[:27].reshape(3, 3, 3, 128, 128).astype(F32)]
    reshape x3 -> x0, local copies, waits for them, and re-layouts: 0.87 us -> none  [the longest x2 0.86 us: body(): vol = jnp.transpose(volume, (1, 0, 2, 3)).reshape(4, 4, 256)]
where the time goes in v2:
time: 56.8 us; the launch traced here: 56.7 us
  Pallas kernels  56 us (99%)
  between operations  0.64 us (1%)
    pallas_call x1, Pallas kernels, body(): pl.pallas_call(kernel, out_shape=jax.ShapeDtypeStruct((32, 128, 128), BF1...  53.8 us
    pallas_call x1, Pallas kernels, body(): pl.pallas_call(widen, out_shape=(jax.ShapeDtypeStruct((27, 4, 128), F32),...  2.25 us

profile of v2, /device:TPU:1, one launch (start us, length us, event | category | flops | bytes accessed | tf_op | source)
XLA Modules:
  0.0 56.7 jit_solution(6933714209842356922)
XLA Ops:
  0.6 53.8 %conv_backward.1.sums_ref = bf16[32,128,128]{2,1,0:T(8,128)(2,1)} custom-call(bf16[4,4,8,32]{3,2,1,0:T(8,128)(2,1)} %vol_ref.1, bf16[4,8,32,128]{3,2,1,0:T(8,128)(2,1)} %bitcast.6, bf16[4,8,32,128]{3,2,1,0:T(8,128)(2,1)} %bitcast.7, bf16[9,384,128]{2,1,0:T(8,128)(2,1)} %bitcast.5), custom_call_target="tpu_custom_call" | custom-call | tf_op jit(solution)/shard_map/conv_backward/pallas_call | solution.py:457
  54.4 2.3 %widen.1 = (f32[27,4,128]{2,1,0:T(4,128)}, f32[27,128,128]{2,1,0:T(8,128)}) custom-call(bf16[32,128,128]{2,1,0:T(8,128)(2,1)} %conv_backward.1.sums_ref), custom_call_target="tpu_custom_call" | custom-call | tf_op jit(solution)/shard_map/widen/pallas_call | solution.py:491

commit v3 on v2

--- a/solution.py
+++ b/solution.py
@@ -209,7 +209,6 @@
         blocks.append(jnp.where(lane % 32 == 0, 0.0, pltpu.roll(field, 1, 1)))
         blocks.append(field)
         blocks.append(jnp.where(lane % 32 == 31, 0.0, pltpu.roll(field, 255, 1)))
-    fields = jnp.concatenate(blocks, axis=0).astype(BF16)
 
     loads[3].wait()
     one = [[jnp.zeros((8, 128), F32) for _ in range(3)] for _ in range(9)]
@@ -233,10 +232,11 @@
         )
         mask = hid[h].reshape(256, 128).astype(F32) > 0
         grad_hidden = jnp.where(mask, grad, 0.0).astype(BF16)
-        terms = jnp.dot(fields, grad_hidden, preferred_element_type=F32)
+        fields = jnp.concatenate([block[8 * h : 8 * h + 24] for block in blocks], axis=0)
+        terms = jnp.dot(fields.astype(BF16), grad_hidden, preferred_element_type=F32)
         for b in range(9):
             for kh in range(3):
-                first = b * 48 + (h + kh) * 8
+                first = b * 24 + kh * 8
                 one[b][kh] = one[b][kh] + terms[first : first + 8]
         if h == 0:
             x_send(5)
@@ -261,16 +261,14 @@
     place = (ys, zs)
     peers = (y_peer, z_peer)
 
-    def first_copy(k, j):
+    def first_copy(k, o, n):
+        j = (place[k] + o) % 8
         target = dev(j, core, zs, xs) if k == 0 else dev(ys, core, j, xs)
-        return send(
-            first_tx.at[k, j], first_rx.at[k, place[k]],
-            f_ss.at[k, j], f_rs.at[k, place[k]], target,
-        )
+        return send(first_tx.at[k, j], first_rx.at[k, o], f_ss.at[k, n], f_rs.at[k, o], target)
 
     seen = set()
 
-    def first_send(k, j):
+    def first_total(k, j):
         lo = 16 * k + 2 * j
         hi = min(lo + 2, 27)
         for g in range(lo // 3, (hi - 1) // 3 + 1):
@@ -291,25 +289,22 @@
             first_sum[27] = one_total
         first_tx[k, j] = first_sum[lo : lo + 2].astype(BF16)
 
-        @pl.when(place[k] != j)
-        def _():
-            first_copy(k, j).start()
+    last = LIVE[1] - 1
+    last_step = (last + 8 - zs) % 8
+
+    def early(n):
+        return (zs + RING[n]) % 8 < last
 
     def second_copy(k, i):
         at = second.at[k, place[1 - k]]
         return send(at, at, s_ss.at[k, i], s_rs.at[k, i], peers[1 - k][i])
 
     def second_send(k):
-        for s in range(8):
-            @pl.when(place[k] != s)
-            def _(s=s):
-                send(
-                    first_tx.at[k, 0], first_rx.at[k, s], f_ss.at[k, 0], f_rs.at[k, s], other
-                ).wait_recv()
-
+        for n in range(7):
+            first_copy(k, RING[n], n).wait_recv()
         total = first_sum[pl.ds(16 * k + 2 * place[k], 2)]
-        for s in range(8):
-            total = total + jnp.where(place[k] == s, 0.0, first_rx[k, s].astype(F32))
+        for n in range(7):
+            total = total + first_rx[k, RING[n]].astype(F32)
         second[k, place[1 - k]] = total.astype(SUM)
         for i in FAR_FIRST:
             second_copy(k, i).start()
@@ -362,9 +357,15 @@
 
     live = place[1] < LIVE[1]
     for j in range(LIVE[0]):
-        first_send(0, j)
-    for j in range(LIVE[1]):
-        first_send(1, j)
+        first_total(0, j)
+    for n in FAR_FIRST:
+        first_copy(0, RING[n], n).start()
+    for j in range(last):
+        first_total(1, j)
+    for n in FAR_FIRST:
+        pl.when(early(n))(lambda n=n: first_copy(1, RING[n], n).start())
+    first_total(1, last)
+    pl.when(zs != last)(lambda: first_copy(1, last_step, 7).start())
     second_send(0)
     pl.when(live)(lambda: second_send(1))
 
@@ -390,11 +391,11 @@
     spread(0)
     spread(1)
 
-    for k in range(2):
-        for j in range(LIVE[k]):
-            @pl.when(place[k] != j)
-            def _(k=k, j=j):
-                first_copy(k, j).wait_send()
+    for n in range(7):
+        first_copy(0, RING[n], n).wait_send()
+    for n in range(7):
+        pl.when(early(n))(lambda n=n: first_copy(1, RING[n], n).wait_send())
+    pl.when(zs != last)(lambda: first_copy(1, last_step, 7).wait_send())
 
     def second_left(k):
         for i in range(7):
@@ -427,23 +428,17 @@
         cg_copy(k, 1).wait_send()
 
 
-def widen(sums_ref, one_ref, two_ref, sums, one, two, sem):
-    ins = []
-    for n in range(4):
-        t = slice(7 * n, 7 * n + 7)
-        ins.append(pltpu.make_async_copy(sums_ref.at[t], sums.at[t], sem.at[n]))
-        ins[n].start()
+def widen(sums_ref, one_ref, two_ref, one, two, sem):
     outs = []
     for n in range(4):
-        ins[n].wait()
         t = slice(7 * n, min(7 * n + 7, 27))
-        two[t] = sums[t].astype(F32)
-        outs.append(pltpu.make_async_copy(two.at[t], two_ref.at[t], sem.at[4 + n]))
+        two[t] = sums_ref[t].astype(F32)
+        outs.append(pltpu.make_async_copy(two.at[t], two_ref.at[t], sem.at[n]))
         outs[n].start()
-    rows = sums[27].astype(F32)
+    rows = sums_ref[27].astype(F32)
     for n in range(27):
         one[n] = rows[4 * n : 4 * n + 4]
-    outs.append(pltpu.make_async_copy(one, one_ref, sem.at[8]))
+    outs.append(pltpu.make_async_copy(one, one_ref, sem.at[4]))
     outs[4].start()
     for c in outs:
         c.wait()
@@ -484,25 +479,24 @@
             dma((2, 3)), dma((2, 3)), dma((2, 2)), dma((2, 2)),
         ],
         compiler_params=pltpu.CompilerParams(
-            collective_id=0, has_side_effects=True, vmem_limit_bytes=60 * 1024 * 1024
+            collective_id=0, has_side_effects=True, vmem_limit_bytes=44 * 1024 * 1024
         ),
         name="conv_backward",
-    )(volume, hid, grad, weights)
+    )(*[pltpu.with_memory_space_constraint(x, pltpu.HBM) for x in (volume, hid, grad, weights)])
     one, two = pl.pallas_call(
         widen,
         out_shape=(
             jax.ShapeDtypeStruct((27, 4, 128), F32),
             jax.ShapeDtypeStruct((27, 128, 128), F32),
         ),
-        in_specs=[pl.BlockSpec(memory_space=pl.ANY)],
+        in_specs=[pl.BlockSpec(memory_space=pltpu.VMEM)],
         out_specs=(pl.BlockSpec(memory_space=pl.ANY),) * 2,
         scratch_shapes=[
-            pltpu.VMEM((TAPS, 128, 128), BF16),
             pltpu.VMEM((27, 4, 128), F32),
             pltpu.VMEM((27, 128, 128), F32),
-            dma((9,)),
+            dma((5,)),
         ],
-        compiler_params=pltpu.CompilerParams(vmem_limit_bytes=60 * 1024 * 1024),
+        compiler_params=pltpu.CompilerParams(vmem_limit_bytes=8 * 1024 * 1024),
         name="widen",
     )(out)
     return (one.reshape(3, 3, 3, 4, 128), two.reshape(3, 3, 3, 128, 128))

time: 56.8 us -> 54.4 us (0.958)
  Pallas kernels: 56 us -> 53.7 us
    pallas_call x1, Pallas kernels: 53.8 us -> 52.4 us  [body(): pl.pallas_call(kernel, out_shape=jax.ShapeDtypeStruct((32, 128, 128), BF1...]
    pallas_call x1, Pallas kernels: 2.25 us -> 1.28 us  [body(): pl.pallas_call(widen, out_shape=(jax.ShapeDtypeStruct((27, 4, 128), F32),...]
where the time goes in v3:
time: 54.4 us; the launch traced here: 54.3 us
  Pallas kernels  53.7 us (99%)
  between operations  0.64 us (1%)
    pallas_call x1, Pallas kernels, body(): pl.pallas_call(kernel, out_shape=jax.ShapeDtypeStruct((32, 128, 128), BF1...  52.4 us
    pallas_call x1, Pallas kernels, body(): pl.pallas_call(widen, out_shape=(jax.ShapeDtypeStruct((27, 4, 128), F32),...  1.28 us

profile of v3, /device:TPU:1, one launch (start us, length us, event | category | flops | bytes accessed | tf_op | source)
XLA Modules:
  0.0 54.3 jit_solution(154299076236457650)
XLA Ops:
  0.6 52.4 %conv_backward.1.sums_ref = bf16[32,128,128]{2,1,0:T(8,128)(2,1)S(1)} custom-call(bf16[4,4,8,32]{3,2,1,0:T(8,128)(2,1)} %vol_ref.1, bf16[4,8,32,128]{3,2,1,0:T(8,128)(2,1)} %bitcast.6, bf16[4,8,32,128]{3,2,1,0:T(8,128)(2,1)} %bitcast.7, bf16[9,384,128]{2,1,0:T(8,128)(2,1)} %bitcast.5), custom_call_target="tpu_custom_call" | custom-call | tf_op jit(solution)/shard_map/conv_backward/pallas_call | solution.py:452
  53.0 1.3 %widen.1 = (f32[27,4,128]{2,1,0:T(4,128)}, f32[27,128,128]{2,1,0:T(8,128)}) custom-call(bf16[32,128,128]{2,1,0:T(8,128)(2,1)S(1)} %conv_backward.1.sums_ref), custom_call_target="tpu_custom_call" | custom-call | tf_op jit(solution)/shard_map/widen/pallas_call | solution.py:486

commit v4 on v3

--- a/solution.py
+++ b/solution.py
@@ -15,7 +15,8 @@
 RING = (1, 7, 2, 6, 3, 5, 4)
 FAR_FIRST = (6, 5, 4, 3, 2, 1, 0)
 LIVE = (8, 6)
-SUM = F32
+SUM = BF16
+PARTS = ((0, 0, 8), (1, 0, 5), (1, 5, 6))
 ONE_STEPS = ((1, 2), (0, 2), (1, 1), (1, 3), (0, 1), (0, 3), (1, 0))
 
 
@@ -30,7 +31,7 @@
 def kernel(
     vol_ref, hid_ref, go_ref, w_ref, out_ref,
     ext, vols, vol_raw, vol_rows, vol_flat, hid, w, act_t, part, core_rx, x_tx, x_rx,
-    one_tx, one_rx, first_tx, first_rx, first_sum, second, stage,
+    one_rx, first_tx, first_rx, first_sum, second, stage,
     load_sem, halo_ss, halo_rs, core_ss, core_rs, x_ss, x_rs, o_ss, o_rs, f_ss, f_rs, s_ss, s_rs,
     g_ss, g_rs, xg_ss, xg_rs, cg_ss, cg_rs,
 ):
@@ -52,6 +53,12 @@
     y_peer = [dev((ys + i) % NY, core, zs, xs) for i in RING]
     z_peer = [dev(ys, core, (zs + i) % NZ, xs) for i in RING]
 
+    barrier = pltpu.get_barrier_semaphore()
+    greet = [p[i] for i in FAR_FIRST for p in (z_peer, y_peer)]
+    greet += cross_peer + x_peer + [near(s) for s in SIDES]
+    for d in greet:
+        pl.semaphore_signal(barrier, inc=1, device_id=d, device_id_type=MESH)
+
     loads = [
         pltpu.make_async_copy(vol_ref, vol_raw, load_sem.at[0]),
         pltpu.make_async_copy(hid_ref, hid, load_sem.at[1]),
@@ -60,11 +67,6 @@
     ]
     for c in loads:
         c.start()
-
-    barrier = pltpu.get_barrier_semaphore()
-    greet = [near(s) for s in SIDES] + x_peer + cross_peer + y_peer + z_peer
-    for d in greet:
-        pl.semaphore_signal(barrier, inc=1, device_id=d, device_id_type=MESH)
 
     def send(src, dst, ss, rs, device):
         c = pltpu.make_async_remote_copy(
@@ -249,13 +251,12 @@
         for kh in range(3):
             first = (kh * 9 + b) * 4
             part[27, first : first + 4, :] = one[b][kh][0:4]
-    one_tx[...] = part[27].astype(BF16)
     one_copies = []
     for i, (c, step) in enumerate(ONE_STEPS):
         half = core if c == 0 else 1 - core
         rows = pl.ds(pl.multiple_of(half * 64 + (xs + step) % NX * 16, 16), 16)
         device = other if step == 0 else (cross_peer if c else x_peer)[X_STEPS.index(step)]
-        one_copies.append(send(one_tx.at[rows], one_rx.at[i], o_ss.at[i], o_rs.at[i], device))
+        one_copies.append(send(part.at[27, rows], one_rx.at[i], o_ss.at[i], o_rs.at[i], device))
         one_copies[i].start()
 
     place = (ys, zs)
@@ -285,7 +286,7 @@
             one_total = part[27, own_rows]
             for i in range(7):
                 one_copies[i].wait_recv()
-                one_total = one_total + one_rx[i].astype(F32)
+                one_total = one_total + one_rx[i]
             first_sum[27] = one_total
         first_tx[k, j] = first_sum[lo : lo + 2].astype(BF16)
 
@@ -310,9 +311,17 @@
             second_copy(k, i).start()
 
     def gather_copy(k, i):
-        return send(
-            stage.at[0, k, 0, 0], stage.at[0, k, 0, 1 + i], g_ss.at[k, i], g_rs.at[k, i], peers[k][i]
-        )
+        if k == 0:
+            return send(
+                stage.at[0, 0, 0, 0], stage.at[0, 0, 0, 1 + i],
+                g_ss.at[0, i], g_rs.at[0, i], y_peer[i],
+            )
+        at = stage.at[0, 1, 0, zs]
+        return send(at, at, g_ss.at[1, i], g_rs.at[1, zs], z_peer[i])
+
+    def gathered(j):
+        at = stage.at[0, 1, 0, j]
+        pl.when(zs != j)(lambda: send(at, at, g_ss.at[1, 0], g_rs.at[1, j], other).wait_recv())
 
     def finish(k):
         for i in range(7):
@@ -320,40 +329,55 @@
         total = second[k, 0].astype(F32)
         for s in range(1, 8):
             total = total + second[k, s].astype(F32)
-        stage[0, k, 0, 0] = total.astype(BF16)
+        stage[0, k, 0, k * zs] = total.astype(BF16)
 
     def gather(k):
         for i in FAR_FIRST:
             gather_copy(k, i).start()
 
-    def xg_copy(k, i):
+    def xg_copy(p, i):
+        k, lo, hi = PARTS[p]
         return send(
-            stage.at[0, k, 0], stage.at[0, k, 1 + i], xg_ss.at[k, i], xg_rs.at[k, i], x_peer[i]
-        )
-
-    def cg_copy(k, m):
+            stage.at[0, k, 0, lo:hi], stage.at[0, k, 1 + i, lo:hi],
+            xg_ss.at[p, i], xg_rs.at[p, i], x_peer[i],
+        )
+
+    def cg_copy(p, m):
+        k, lo, hi = PARTS[p]
         r = slice(1, 4) if m else slice(0, 1)
-        return send(stage.at[0, k, r], stage.at[1, k, r], cg_ss.at[k, m], cg_rs.at[k, m], other)
-
-    def spread(k):
-        for i in range(7):
-            gather_copy(k, i).wait_recv()
+        return send(
+            stage.at[0, k, r, lo:hi], stage.at[1, k, r, lo:hi],
+            cg_ss.at[p, m], cg_rs.at[p, m], other,
+        )
+
+    def spread(p):
+        k, lo, hi = PARTS[p]
+        if k == 0:
+            for i in range(7):
+                gather_copy(0, i).wait_recv()
+        else:
+            for j in range(lo, hi):
+                gathered(j)
         for i in range(3):
-            xg_copy(k, i).start()
-        cg_copy(k, 0).start()
-
-    def forward(k):
+            xg_copy(p, i).start()
+        cg_copy(p, 0).start()
+
+    def forward(p):
         for i in range(3):
-            xg_copy(k, i).wait_recv()
-        cg_copy(k, 1).start()
-
-    def put(c, k, r):
+            xg_copy(p, i).wait_recv()
+        cg_copy(p, 1).start()
+
+    def put(c, p, r):
+        k, lo, hi = PARTS[p]
         half = core if c == 0 else 1 - core
         x = xs if r == 0 else (xs + NX - X_STEPS[r - 1]) % NX
         rows = pl.ds(pl.multiple_of(half * 64 + x * 16, 16), 16)
-        for s in range(8):
-            j = place[k] if s == 0 else (place[k] + 8 - RING[s - 1]) % 8
-            out_ref[pl.ds(16 * k + 2 * j, 2), rows] = stage[c, k, r, s]
+        for s in range(lo, hi):
+            if k == 0:
+                j = ys if s == 0 else (ys + 8 - RING[s - 1]) % 8
+                out_ref[pl.ds(2 * j, 2), rows] = stage[c, 0, r, s]
+            else:
+                out_ref[16 + 2 * s : 18 + 2 * s, rows] = stage[c, 1, r, s]
 
     live = place[1] < LIVE[1]
     for j in range(LIVE[0]):
@@ -377,12 +401,7 @@
     finish(0)
     gather(0)
     pl.when(live)(lambda: finish(1))
-
-    @pl.when(place[1] >= LIVE[1])
-    def _():
-        stage[0, 1, 0, 0] = jnp.zeros((2, 16, 128), BF16)
-
-    gather(1)
+    pl.when(live)(lambda: gather(1))
     for g in range(9):
         for c in x_copies[g]:
             c.wait_send()
@@ -403,29 +422,31 @@
 
     second_left(0)
     pl.when(live)(lambda: second_left(1))
-    for k in range(2):
-        put(0, k, 0)
+    def gather_left(k):
         for i in range(7):
             gather_copy(k, i).wait_send()
-    forward(0)
-    for r in range(1, 4):
-        put(0, 0, r)
-    cg_copy(0, 0).wait_recv()
-    put(1, 0, 0)
-    forward(1)
-    for r in range(1, 4):
-        put(0, 1, r)
-    cg_copy(1, 0).wait_recv()
-    put(1, 1, 0)
-    for k in range(2):
+
+    gather_left(0)
+    pl.when(live)(lambda: gather_left(1))
+    put(0, 0, 0)
+    put(0, 1, 0)
+    spread(2)
+    put(0, 2, 0)
+    for p in range(3):
+        forward(p)
+        for r in range(1, 4):
+            put(0, p, r)
+        cg_copy(p, 0).wait_recv()
+        put(1, p, 0)
+    for p in range(3):
         for i in range(3):
-            xg_copy(k, i).wait_send()
-        cg_copy(k, 0).wait_send()
-    for k in range(2):
-        cg_copy(k, 1).wait_recv()
+            xg_copy(p, i).wait_send()
+        cg_copy(p, 0).wait_send()
+    for p in range(3):
+        cg_copy(p, 1).wait_recv()
         for r in range(1, 4):
-            put(1, k, r)
-        cg_copy(k, 1).wait_send()
+            put(1, p, r)
+        cg_copy(p, 1).wait_send()
 
 
 def widen(sums_ref, one_ref, two_ref, one, two, sem):
@@ -451,7 +472,7 @@
     dma = pltpu.SemaphoreType.DMA
     out = pl.pallas_call(
         kernel,
-        out_shape=jax.ShapeDtypeStruct((32, 128, 128), BF16),
+        out_shape=jax.ShapeDtypeStruct((TAPS, 128, 128), BF16),
         in_specs=[pl.BlockSpec(memory_space=pltpu.HBM)] * 4,
         out_specs=pl.BlockSpec(memory_space=pltpu.VMEM),
         scratch_shapes=[
@@ -467,8 +488,7 @@
             pltpu.VMEM((27, 64, 128), F32),
             pltpu.VMEM((27, 64, 128), BF16),
             pltpu.VMEM((3, 27, 16, 128), BF16),
-            pltpu.VMEM((128, 128), BF16),
-            pltpu.VMEM((7, 16, 128), BF16),
+            pltpu.VMEM((7, 16, 128), F32),
             pltpu.VMEM((2, 8, 2, 16, 128), BF16),
             pltpu.VMEM((2, 8, 2, 16, 128), BF16),
             pltpu.VMEM((TAPS, 16, 128), F32),
@@ -476,7 +496,7 @@
             pltpu.VMEM((2, 2, 4, 8, 2, 16, 128), BF16),
             dma((4,)), dma((16,)), dma((16,)), dma((9,)), dma((9,)), dma((9, 3)), dma((9, 3)),
             dma((7,)), dma((7,)), dma((2, 8)), dma((2, 8)), dma((2, 7)), dma((2, 7)), dma((2, 7)), dma((2, 7)),
-            dma((2, 3)), dma((2, 3)), dma((2, 2)), dma((2, 2)),
+            dma((3, 3)), dma((3, 3)), dma((3, 2)), dma((3, 2)),
         ],
         compiler_params=pltpu.CompilerParams(
             collective_id=0, has_side_effects=True, vmem_limit_bytes=44 * 1024 * 1024

time: 54.4 us -> 53.9 us (level)
  Pallas kernels: 53.7 us -> 53.1 us
    pallas_call x1, Pallas kernels: 52.4 us -> 51.9 us  [body(): pl.pallas_call(kernel, out_shape=jax.ShapeDtypeStruct((TAPS, 128, 128), B...]
where the time goes in v4:
time: 53.9 us; the launch traced here: 53.8 us
  Pallas kernels  53.1 us (99%)
  between operations  0.64 us (1%)
    pallas_call x1, Pallas kernels, body(): pl.pallas_call(kernel, out_shape=jax.ShapeDtypeStruct((TAPS, 128, 128), B...  51.9 us
    pallas_call x1, Pallas kernels, body(): pl.pallas_call(widen, out_shape=(jax.ShapeDtypeStruct((27, 4, 128), F32),...  1.28 us

profile of v4, /device:TPU:1, one launch (start us, length us, event | category | flops | bytes accessed | tf_op | source)
XLA Modules:
  0.0 53.8 jit_solution(7902818802001173991)
XLA Ops:
  0.6 51.9 %conv_backward.1.sums_ref = bf16[28,128,128]{2,1,0:T(8,128)(2,1)S(1)} custom-call(bf16[4,4,8,32]{3,2,1,0:T(8,128)(2,1)} %vol_ref.1, bf16[4,8,32,128]{3,2,1,0:T(8,128)(2,1)} %bitcast.6, bf16[4,8,32,128]{3,2,1,0:T(8,128)(2,1)} %bitcast.7, bf16[9,384,128]{2,1,0:T(8,128)(2,1)} %bitcast.5), custom_call_target="tpu_custom_call" | custom-call | tf_op jit(solution)/shard_map/conv_backward/pallas_call | solution.py:473
  52.5 1.3 %widen.1 = (f32[27,4,128]{2,1,0:T(4,128)}, f32[27,128,128]{2,1,0:T(8,128)}) custom-call(bf16[28,128,128]{2,1,0:T(8,128)(2,1)S(1)} %conv_backward.1.sums_ref), custom_call_target="tpu_custom_call" | custom-call | tf_op jit(solution)/shard_map/widen/pallas_call | solution.py:506

commit v5 on v4

--- a/solution.py
+++ b/solution.py
@@ -15,7 +15,7 @@
 RING = (1, 7, 2, 6, 3, 5, 4)
 FAR_FIRST = (6, 5, 4, 3, 2, 1, 0)
 LIVE = (8, 6)
-SUM = BF16
+SUMS = (F32, BF16)
 PARTS = ((0, 0, 8), (1, 0, 5), (1, 5, 6))
 ONE_STEPS = ((1, 2), (0, 2), (1, 1), (1, 3), (0, 1), (0, 3), (1, 0))
 
@@ -31,7 +31,7 @@
 def kernel(
     vol_ref, hid_ref, go_ref, w_ref, out_ref,
     ext, vols, vol_raw, vol_rows, vol_flat, hid, w, act_t, part, core_rx, x_tx, x_rx,
-    one_rx, first_tx, first_rx, first_sum, second, stage,
+    one_rx, first_tx, first_rx, first_sum, second_0, second_1, stage,
     load_sem, halo_ss, halo_rs, core_ss, core_rs, x_ss, x_rs, o_ss, o_rs, f_ss, f_rs, s_ss, s_rs,
     g_ss, g_rs, xg_ss, xg_rs, cg_ss, cg_rs,
 ):
@@ -296,8 +296,10 @@
     def early(n):
         return (zs + RING[n]) % 8 < last
 
+    second = (second_0, second_1)
+
     def second_copy(k, i):
-        at = second.at[k, place[1 - k]]
+        at = second[k].at[place[1 - k]]
         return send(at, at, s_ss.at[k, i], s_rs.at[k, i], peers[1 - k][i])
 
     def second_send(k):
@@ -306,7 +308,7 @@
         total = first_sum[pl.ds(16 * k + 2 * place[k], 2)]
         for n in range(7):
             total = total + first_rx[k, RING[n]].astype(F32)
-        second[k, place[1 - k]] = total.astype(SUM)
+        second[k][place[1 - k]] = total.astype(SUMS[k])
         for i in FAR_FIRST:
             second_copy(k, i).start()
 
@@ -326,9 +328,9 @@
     def finish(k):
         for i in range(7):
             second_copy(k, i).wait_recv()
-        total = second[k, 0].astype(F32)
+        total = second[k][0].astype(F32)
         for s in range(1, 8):
-            total = total + second[k, s].astype(F32)
+            total = total + second[k][s].astype(F32)
         stage[0, k, 0, k * zs] = total.astype(BF16)
 
     def gather(k):
@@ -492,7 +494,8 @@
             pltpu.VMEM((2, 8, 2, 16, 128), BF16),
             pltpu.VMEM((2, 8, 2, 16, 128), BF16),
             pltpu.VMEM((TAPS, 16, 128), F32),
-            pltpu.VMEM((2, 8, 2, 16, 128), SUM),
+            pltpu.VMEM((8, 2, 16, 128), SUMS[0]),
+            pltpu.VMEM((8, 2, 16, 128), SUMS[1]),
             pltpu.VMEM((2, 2, 4, 8, 2, 16, 128), BF16),
             dma((4,)), dma((16,)), dma((16,)), dma((9,)), dma((9,)), dma((9, 3)), dma((9, 3)),
             dma((7,)), dma((7,)), dma((2, 8)), dma((2, 8)), dma((2, 7)), dma((2, 7)), dma((2, 7)), dma((2, 7)),

time: 53.9 us -> 54 us (level)
  no operation moved by 1% of the time
where the time goes in v5:
time: 54 us; the launch traced here: 53.9 us
  Pallas kernels  53.2 us (99%)
  between operations  0.64 us (1%)
    pallas_call x1, Pallas kernels, body(): pl.pallas_call(kernel, out_shape=jax.ShapeDtypeStruct((TAPS, 128, 128), B...  51.9 us
    pallas_call x1, Pallas kernels, body(): pl.pallas_call(widen, out_shape=(jax.ShapeDtypeStruct((27, 4, 128), F32),...  1.28 us

profile of v5, /device:TPU:1, one launch (start us, length us, event | category | flops | bytes accessed | tf_op | source)
XLA Modules:
  0.0 53.9 jit_solution(16990628502434238326)
XLA Ops:
  0.6 51.9 %conv_backward.1.sums_ref = bf16[28,128,128]{2,1,0:T(8,128)(2,1)S(1)} custom-call(bf16[4,4,8,32]{3,2,1,0:T(8,128)(2,1)} %vol_ref.1, bf16[4,8,32,128]{3,2,1,0:T(8,128)(2,1)} %bitcast.6, bf16[4,8,32,128]{3,2,1,0:T(8,128)(2,1)} %bitcast.7, bf16[9,384,128]{2,1,0:T(8,128)(2,1)} %bitcast.5), custom_call_target="tpu_custom_call" | custom-call | tf_op jit(solution)/shard_map/conv_backward/pallas_call | solution.py:475
  52.6 1.3 %widen.1 = (f32[27,4,128]{2,1,0:T(4,128)}, f32[27,128,128]{2,1,0:T(8,128)}) custom-call(bf16[28,128,128]{2,1,0:T(8,128)(2,1)S(1)} %conv_backward.1.sums_ref), custom_call_target="tpu_custom_call" | custom-call | tf_op jit(solution)/shard_map/widen/pallas_call | solution.py:509
